TPU v7x, 512 devices: a whole 4x8x8 slice. The times are simulated.
512 devices in a mesh: seq: 128 (over y, z, core), head: 4 (over x).
Axes of the slice: x: 4, y: 8, z: 8, core: 2. Of those that a mesh axis runs over, the one named last changes fastest.
Arguments:
- queries: bfloat16 [131072, 512], P('seq', 'head'), may hold values from -6 to 6
- keys: bfloat16 [131072, 512], P('seq', 'head'), may hold values from -6 to 6
- values: bfloat16 [131072, 512], P('seq', 'head'), may hold values from -6 to 6
- out_grad: bfloat16 [131072, 512], P('seq', 'head'), may hold values from -6 to 6
- lengths: int32 [64], replicated, may hold values from 1 to 3072, 131072 in all
- w_proj: bfloat16 [3, 512, 512], P(None, None, 'head'), may hold values from -0.25 to 0.25
Outputs:
- d_input: float32 [131072, 512], P(('seq', 'head'))
Inputs may be any that keep to these rules, and one draw needn't show every extreme that they name: The lengths sum to 131072; the longest is exactly 3072.
All inputs are finite; a program needn't handle non-finite values.
Results may differ from a plain program's by a relative error of at most 0.006.
Values may be sent and summed in bfloat16 or wider, within the bound.
A program may use at most 64 MiB of HBM per device.

v0:
```python
import math

import jax
import jax.numpy as jnp
from jax import lax
from jax.sharding import PartitionSpec as P

LAGS = 4
MAXLEN = 3072


def from_behind(value, axis, by):
    count = lax.axis_size(axis)
    pairs = [(i, i + by) for i in range(count) if 0 <= i + by < count]
    return lax.ppermute(value, axis, pairs)


def user_of(positions, user_ends):
    return jnp.sum((user_ends[None, :] <= positions[:, None]).astype(jnp.int32), axis=1)


def tile_task(query_side, key_side, query_start, key_start, user_ends):
    tile_rows = query_side.shape[1]
    head_width = query_side.shape[2]
    score_scale = head_width ** (-0.5)
    norm_factor = 1.0 / math.sqrt(MAXLEN)
    offsets = lax.iota(jnp.int32, tile_rows)
    query_pos = query_start + offsets
    key_pos = key_start + offsets
    query_user = user_of(query_pos, user_ends)
    key_user = user_of(key_pos, user_ends)
    visible = (key_pos[None, :] <= query_pos[:, None]) & (query_user[:, None] == key_user[None, :])
    scores = (
        jnp.einsum("qh,kh->qk", query_side[0], key_side[0], preferred_element_type=jnp.float32)
        * score_scale
    )
    gate_prob = jax.nn.sigmoid(scores)
    weights = jnp.where(visible, scores * gate_prob * norm_factor, 0.0).astype(jnp.bfloat16)
    d_weights = jnp.einsum(
        "qh,kh->qk", query_side[1], key_side[1], preferred_element_type=jnp.float32
    )
    d_scores = jnp.where(
        visible, d_weights * gate_prob * (1.0 + scores * (1.0 - gate_prob)) * norm_factor, 0.0
    ).astype(jnp.bfloat16)
    query_grad = (
        jnp.dot(d_scores, key_side[0], preferred_element_type=jnp.float32) * score_scale
    ).astype(jnp.bfloat16)
    key_grad = (
        jnp.einsum("qk,qh->kh", d_scores, query_side[0], preferred_element_type=jnp.float32)
        * score_scale
    ).astype(jnp.bfloat16)
    value_grad = jnp.einsum(
        "qk,qh->kh", weights, query_side[1], preferred_element_type=jnp.float32
    ).astype(jnp.bfloat16)
    return (query_grad, jnp.stack([key_grad, value_grad]))


def shards(queries, keys, values, out_grad, lengths, w_proj):
    tile_rows = queries.shape[0]
    device_count = lax.axis_size("seq")
    my_index = lax.axis_index("seq")
    user_ends = jnp.cumsum(lengths)
    all_tokens = tile_rows * device_count
    tile_start = my_index * tile_rows
    query_pair = jnp.stack([queries, out_grad])
    key_pair = jnp.stack([keys, values])

    def last_user(position):
        return jnp.sum((user_ends <= position).astype(jnp.int32))

    def zero_parts():
        return (jnp.zeros_like(queries), jnp.zeros_like(key_pair))

    query_grad, pair_grad = tile_task(query_pair, key_pair, tile_start, tile_start, user_ends)
    query_total = query_grad.astype(jnp.float32)
    pair_total = pair_grad.astype(jnp.float32)
    for offset in range(1, LAGS):
        arrived = from_behind(key_pair, "seq", offset)
        guarded_key_start = tile_start - offset * tile_rows
        key_side = arrived
        shared = (
            (guarded_key_start >= 0)
            & (tile_start < all_tokens)
            & (last_user(tile_start) == last_user(guarded_key_start + tile_rows - 1))
        )
        query_part, pair_part = lax.cond(
            shared,
            lambda: tile_task(query_pair, key_side, tile_start, guarded_key_start, user_ends),
            zero_parts,
        )
        query_total = query_total + query_part.astype(jnp.float32)
        returned = from_behind(pair_part, "seq", -offset)
        pair_total = pair_total + returned.astype(jnp.float32)
    stacked_grads = jnp.stack([query_total, pair_total[0], pair_total[1]]).astype(jnp.bfloat16)
    return lax.psum_scatter(
        jnp.einsum("crh,cdh->rd", stacked_grads, w_proj, preferred_element_type=jnp.float32),
        "head",
        scatter_dimension=0,
        tiled=True,
    )


def solution(mesh):
    return jax.shard_map(
        shards,
        mesh=mesh,
        in_specs=(
            P("seq", "head"),
            P("seq", "head"),
            P("seq", "head"),
            P("seq", "head"),
            P(),
            P(None, None, "head"),
        ),
        out_specs=P(("seq", "head"), None),
        check_vma=False,
    )
```

profile of v0, /device:TPU:1, one launch (start us, length us, event | category | flops | bytes accessed | tf_op | source)
XLA Modules:
  0.0 133.2 jit_solution(17998723188469048668)
XLA Ops:
  6.5 1.9 %pad_maximum_fusion.3 = bf16[2,1024,128]{2,1,0:T(8,128)(2,1)} fusion(bf16[1,1024,128]{2,1,0:T(8,128)(2,1)} %bitcast.76, bf16[1,1024,128]{2,1,0:T(8,128)(2,1)} %bitcast.75), kind=kLoop, calls=%fused_computation.105 | loop fusion | flops 262144 | bytes 1048576 | tf_op jit(solution)/shard_map/stack | solution.py:66
  8.5 7.2 %collective-permute-start.2 = (bf16[2,1024,128]{2,1,0:T(8,128)(2,1)}, bf16[2,1024,128]{2,1,0:T(8,128)(2,1)S(1)}, u32[]{:S(2)}, u32[]{:S(2)}) collective-permute-start(bf16[2,1024,128]{2,1,0:T(8,128)(2,1)} %pad_maximum_fusion.3), channel_id=1, source_target_pairs={{0,12},{4,16},{8,20},{12,24},{16,28},{20,32},{24,36},{28,40},{32,4... | collective-permute-start | bytes 1572872 | tf_op jit(solution)/shard_map/ppermute | solution.py:15
  15.7 4.8 %collective-permute-start.1 = (bf16[2,1024,128]{2,1,0:T(8,128)(2,1)}, bf16[2,1024,128]{2,1,0:T(8,128)(2,1)}, u32[]{:S(2)}, u32[]{:S(2)}) collective-permute-start(bf16[2,1024,128]{2,1,0:T(8,128)(2,1)} %pad_maximum_fusion.3), channel_id=1, source_target_pairs={{0,8},{4,12},{8,16},{12,20},{16,24},{20,28},{24,32},{28,36},{32,40... | collective-permute-start | bytes 1572872 | tf_op jit(solution)/shard_map/ppermute | solution.py:15
  20.5 1.9 %collective-permute-start = (bf16[2,1024,128]{2,1,0:T(8,128)(2,1)}, bf16[2,1024,128]{2,1,0:T(8,128)(2,1)}, u32[]{:S(2)}, u32[]{:S(2)}) collective-permute-start(bf16[2,1024,128]{2,1,0:T(8,128)(2,1)} %pad_maximum_fusion.3), channel_id=1, source_target_pairs={{0,4},{4,8},{8,12},{12,16},{16,20},{20,24},{24,28},{28,32},{32,36}... | collective-permute-start | bytes 1572872 | tf_op jit(solution)/shard_map/ppermute | solution.py:15
  27.9 1.7 %fusion.74 = f32[1024,1024]{1,0:T(8,128)S(1)} fusion(bf16[1024,128]{1,0:T(8,128)(2,1)} %param.12, bf16[1024,128]{1,0:T(8,128)(2,1)} %param.13), kind=kOutput, calls=%fused_computation.123 | convolution fusion | flops 268435456 | bytes 4718592 | tf_op jit(solution)/shard_map/qh,kh->qk/dot_general | solution.py:34
  29.7 3.1 %select_convert_fusion.22 = bf16[1024,1024]{1,0:T(8,128)(2,1)S(1)} fusion(f32[1024,1024]{1,0:T(8,128)S(1)} %fusion.74, bf16[1024,128]{1,0:T(8,128)(2,1)S(1)} %copy-done.8, bf16[1024,128]{1,0:T(8,128)(2,1)S(1)} %copy-done.7, s32[1024]{0:T(1024)S(1)} %convert_reduce_fusion.6, s32[1024]{0:T(1024)S(1)} %iota_add_fusion.6), kind=kOutput, calls=%fused_computation.88 | convolution fusion | flops 284164096 | bytes 6823936 | tf_op jit(solution)/shard_map/qh,kh->qk/dot_general | solution.py:39
  32.8 2.9 %fusion.60 = bf16[1,1024,128]{2,1,0:T(8,128)(2,1)} fusion(bf16[1024,128]{1,0:T(8,128)(2,1)S(1)} %copy-done.8, f32[1024,1024]{1,0:T(8,128)S(1)} %fusion.74, s32[1024]{0:T(1024)S(1)} %convert_reduce_fusion.6, s32[1024]{0:T(1024)S(1)} %iota_add_fusion.6), kind=kOutput, calls=%fused_computation.100 | convolution fusion | flops 280100864 | bytes 4726784 | tf_op jit(solution)/shard_map/qk,qh->kh/dot_general | solution.py:52
  35.7 0.9 conditional.5
  35.7 0.9 broadcast.117
  36.7 1.3 collective-permute-start.5
  38.0 1.1 conditional.4
  39.1 1.3 collective-permute-start.4
  40.4 4.2 %collective-permute-done = bf16[2,1024,128]{2,1,0:T(8,128)(2,1)} collective-permute-done((bf16[2,1024,128]{2,1,0:T(8,128)(2,1)}, bf16[2,1024,128]{2,1,0:T(8,128)(2,1)}, u32[]{:S(2)}, u32[]{:S(2)}) %collective-permute-start) | collective-permute-done | bytes 524320 | tf_op jit(solution)/shard_map/ppermute | solution.py:15
  44.6 10.6 %conditional.3 = (bf16[2,1024,128]{2,1,0:T(8,128)(2,1)S(1)}, f32[1024,128]{1,0:T(8,128)S(1)}) conditional(s32[]{:T(128)} %convert_element_type.145, () %tuple.35, (s32[]{:T(128)}, s32[]{:T(128)}, s32[64]{0:T(128)S(1)}, bf16[2,1024,128]{2,1,0:T(8,128)(2,1)}, bf16[1024,128]{1,0:T(8,128)(2,1)}, /*index=5*/bf16[1024,128]{1,0:T(8,128)(2,1)S(1)}) %tuple.60), branch_computations={%region_4.5_spmd, %region_5.8_spmd} | conditional | flops 1370882048 | bytes 23912756 | solution.py:86
  44.8 1.7 %fusion.8 = f32[1024,1024]{1,0:T(8,128)S(1)} fusion(bf16[1024,128]{1,0:T(8,128)(2,1)S(1)} %get-tuple-element.49, bf16[2,1024,128]{2,1,0:T(8,128)(2,1)} %get-tuple-element.48), kind=kOutput, calls=%fused_computation.15 | convolution fusion | flops 268435456 | bytes 4718592 | tf_op jit(solution)/shard_map/cond/branch_1_fun/qh,kh->qk/dot_general | solution.py:34
  46.4 2.2 %fusion.6 = bf16[1,1024,128]{2,1,0:T(8,128)(2,1)S(1)} fusion(bf16[1024,128]{1,0:T(8,128)(2,1)S(1)} %copy-done.10, f32[1024,1024]{1,0:T(8,128)S(1)} %fusion.8, s32[1024]{0:T(1024)S(1)} %get-tuple-element.75, s32[1024]{0:T(1024)S(1)} %get-tuple-element.85, s32[1024]{0:T(1024)S(1)} %get-tuple-element.74, s32[1024]{0:T(1024)S(1)} %get-tuple-element.84), kind=kOutput, calls=%fused_computation.12 | convolution fusion | flops 280100864 | bytes 4734976 | tf_op jit(solution)/shard_map/cond/branch_1_fun/qk,qh->kh/dot_general | solution.py:52
  48.6 4.1 %select_convert_fusion.1 = bf16[1024,1024]{1,0:T(8,128)(2,1)S(1)} fusion(f32[1024,1024]{1,0:T(8,128)S(1)} %fusion.8, bf16[1024,128]{1,0:T(8,128)(2,1)S(1)} %copy-done.10, s32[1024]{0:T(1024)S(1)} %get-tuple-element.75, s32[1024]{0:T(1024)S(1)} %get-tuple-element.85, s32[1024]{0:T(1024)S(1)} %get-tuple-element.74, s32[1024]{0:T(1024)S(1)} %get-tuple-element.84, ...), kind=kOutput, calls=%fused_computation.1 | convolution fusion | flops 284164096 | bytes 6832128 | tf_op jit(solution)/shard_map/cond/branch_1_fun/qh,kh->qk/dot_general | solution.py:39
  52.7 1.7 %fusion.3 = f32[1024,128]{1,0:T(8,128)S(1)} fusion(bf16[1024,1024]{1,0:T(8,128)(2,1)S(1)} %select_convert_fusion.1, bf16[2,1024,128]{2,1,0:T(8,128)(2,1)} %get-tuple-element.48), kind=kOutput, calls=%fused_computation.9 | convolution fusion | flops 268828672 | bytes 2883584 | tf_op jit(solution)/shard_map/cond/branch_1_fun/dot_general | solution.py:46
  55.2 2.1 %collective-permute-start.3 = (bf16[2,1024,128]{2,1,0:T(8,128)(2,1)S(1)}, bf16[2,1024,128]{2,1,0:T(8,128)(2,1)S(1)}, u32[]{:S(2)}, u32[]{:S(2)}) collective-permute-start(bf16[2,1024,128]{2,1,0:T(8,128)(2,1)S(1)} %get-tuple-element.71), channel_id=1, source_target_pairs={{4,0},{8,4},{12,8},{16,12},{20,16},{24,20},{28,24},{32,28},{36,32}... | collective-permute-start | bytes 1572872 | tf_op jit(solution)/shard_map/ppermute | solution.py:15
  59.6 9.7 %collective-permute-done.4 = bf16[2,1024,128]{2,1,0:T(8,128)(2,1)} collective-permute-done((bf16[2,1024,128]{2,1,0:T(8,128)(2,1)}, bf16[2,1024,128]{2,1,0:T(8,128)(2,1)}, u32[]{:S(2)}, u32[]{:S(2)}) %collective-permute-start.4) | collective-permute-done | bytes 524320 | tf_op jit(solution)/shard_map/ppermute | solution.py:15
  69.3 7.7 %collective-permute-done.3 = bf16[2,1024,128]{2,1,0:T(8,128)(2,1)S(1)} collective-permute-done((bf16[2,1024,128]{2,1,0:T(8,128)(2,1)S(1)}, bf16[2,1024,128]{2,1,0:T(8,128)(2,1)S(1)}, u32[]{:S(2)}, u32[]{:S(2)}) %collective-permute-start.3) | collective-permute-done | bytes 524320 | tf_op jit(solution)/shard_map/ppermute | solution.py:15
  77.0 1.5 %add_convert_fusion = bf16[2,1024,128]{2,1,0:T(8,128)(2,1)S(1)} fusion(bf16[2,1024,128]{2,1,0:T(8,128)(2,1)} %collective-permute-done.5, bf16[2,1024,128]{2,1,0:T(8,128)(2,1)} %collective-permute-done.4, bf16[2,1024,128]{2,1,0:T(8,128)(2,1)S(1)} %collective-permute-done.3, bf16[1,1024,128]{2,1,0:T(8,128)(2,1)S(1)} %copy-done.6, ...), kind=kLoop, calls=%fused_computation.101 | loop fusion | flops 2359296 | bytes 2621440 | tf_op jit(solution)/shard_map/convert.1
  78.5 2.1 %convolution_bitcast_fusion = f32[1024,512]{1,0:T(8,128)} fusion(bf16[3,512,128]{2,1,0:T(8,128)(2,1)S(1)} %copy-done, bf16[2,1024,128]{2,1,0:T(8,128)(2,1)S(1)} %add_convert_fusion, bf16[1,1024,128]{2,1,0:T(8,128)(2,1)S(1)} %fusion.64), kind=kOutput, calls=%fused_computation.92 | convolution fusion | flops 403046400 | bytes 3276800 | tf_op jit(solution)/shard_map/crh,cdh->rd/dot_general | solution.py:96
  80.6 45.8 %reduce-scatter.2.cloned.1.call-done = f32[256,512]{1,0:T(8,128)} async-done(((f32[1024,512]{1,0:T(8,128)}), f32[256,512]{1,0:T(8,128)}) %reduce-scatter.2.cloned.1.call-update) | async-done | bytes 524304 | tf_op jit(solution)/shard_map/reduce_scatter | solution.py:95
  (39 shorter events, 6.0 us)
Async XLA Ops:
  6.5 71.9 %copy-start = (bf16[3,512,128]{2,1,0:T(8,128)(2,1)S(1)}, bf16[3,512,128]{2,1,0:T(8,128)(2,1)}, u32[]{:S(2)}) copy-start(bf16[3,512,128]{2,1,0:T(8,128)(2,1)} %param.17) | copy-start | bytes 1179652
  6.5 23.1 %copy-start.7 = (bf16[1024,128]{1,0:T(8,128)(2,1)S(1)}, bf16[1024,128]{1,0:T(8,128)(2,1)}, u32[]{:S(2)}) copy-start(bf16[1024,128]{1,0:T(8,128)(2,1)} %param.14) | copy-start | bytes 786436
  6.5 119.9 %reduce-scatter.2.cloned.1.call-start = ((), (), s32[]{:S(2)}) async-start(), calls=%async_computation.1 | async-start | bytes 2621440 | tf_op jit(solution)/shard_map/reduce_scatter | solution.py:95
  8.5 27.3 %collective-permute-start.2 = (bf16[2,1024,128]{2,1,0:T(8,128)(2,1)}, bf16[2,1024,128]{2,1,0:T(8,128)(2,1)S(1)}, u32[]{:S(2)}, u32[]{:S(2)}) collective-permute-start(bf16[2,1024,128]{2,1,0:T(8,128)(2,1)} %pad_maximum_fusion.3), channel_id=1, source_target_pairs={{0,12},{4,16},{8,20},{12,24},{16,28},{20,32},{24,36},{28,40},{32,4... | collective-permute-start | bytes 1572872 | tf_op jit(solution)/shard_map/ppermute | solution.py:15
  15.7 22.3 %collective-permute-start.1 = (bf16[2,1024,128]{2,1,0:T(8,128)(2,1)}, bf16[2,1024,128]{2,1,0:T(8,128)(2,1)}, u32[]{:S(2)}, u32[]{:S(2)}) collective-permute-start(bf16[2,1024,128]{2,1,0:T(8,128)(2,1)} %pad_maximum_fusion.3), channel_id=1, source_target_pairs={{0,8},{4,12},{8,16},{12,20},{16,24},{20,28},{24,32},{28,36},{32,40... | collective-permute-start | bytes 1572872 | tf_op jit(solution)/shard_map/ppermute | solution.py:15
  20.5 24.1 %collective-permute-start = (bf16[2,1024,128]{2,1,0:T(8,128)(2,1)}, bf16[2,1024,128]{2,1,0:T(8,128)(2,1)}, u32[]{:S(2)}, u32[]{:S(2)}) collective-permute-start(bf16[2,1024,128]{2,1,0:T(8,128)(2,1)} %pad_maximum_fusion.3), channel_id=1, source_target_pairs={{0,4},{4,8},{8,12},{12,16},{16,20},{20,24},{24,28},{28,32},{32,36}... | collective-permute-start | bytes 1572872 | tf_op jit(solution)/shard_map/ppermute | solution.py:15
  27.8 1.9 %copy-start.8 = (bf16[1024,128]{1,0:T(8,128)(2,1)S(1)}, bf16[1024,128]{1,0:T(8,128)(2,1)}, u32[]{:S(2)}) copy-start(bf16[1024,128]{1,0:T(8,128)(2,1)} %param.15) | copy-start | bytes 786436
  32.8 3.0 %copy-start.1 = (bf16[1024,128]{1,0:T(8,128)(2,1)S(1)}, bf16[1024,128]{1,0:T(8,128)(2,1)}, u32[]{:S(2)}) copy-start(bf16[1024,128]{1,0:T(8,128)(2,1)} %param.12) | copy-start | bytes 786436
  36.7 22.9 %collective-permute-start.5 = (bf16[2,1024,128]{2,1,0:T(8,128)(2,1)}, bf16[2,1024,128]{2,1,0:T(8,128)(2,1)}, u32[]{:S(2)}, u32[]{:S(2)}) collective-permute-start(bf16[2,1024,128]{2,1,0:T(8,128)(2,1)} %get-tuple-element.73), channel_id=1, source_target_pairs={{12,0},{16,4},{20,8},{24,12},{28,16},{32,20},{36,24},{40,28},{44,3... | collective-permute-start | bytes 1572872 | tf_op jit(solution)/shard_map/ppermute | solution.py:15
  39.1 5.5 %copy-start.3 = (f32[1024,128]{1,0:T(8,128)}, f32[1024,128]{1,0:T(8,128)S(1)}, u32[]{:S(2)}) copy-start(f32[1024,128]{1,0:T(8,128)S(1)} %get-tuple-element.69) | copy-start | bytes 1572868
  39.1 30.2 %collective-permute-start.4 = (bf16[2,1024,128]{2,1,0:T(8,128)(2,1)}, bf16[2,1024,128]{2,1,0:T(8,128)(2,1)}, u32[]{:S(2)}, u32[]{:S(2)}) collective-permute-start(bf16[2,1024,128]{2,1,0:T(8,128)(2,1)} %get-tuple-element.72), channel_id=1, source_target_pairs={{8,0},{12,4},{16,8},{20,12},{24,16},{28,20},{32,24},{36,28},{40,32... | collective-permute-start | bytes 1572872 | tf_op jit(solution)/shard_map/ppermute | solution.py:15
  44.6 12.7 %copy-start.2 = (bf16[1024,128]{1,0:T(8,128)(2,1)S(1)}, bf16[1024,128]{1,0:T(8,128)(2,1)}, u32[]{:S(2)}) copy-start(bf16[1024,128]{1,0:T(8,128)(2,1)} %param.13) | copy-start | bytes 786436
  44.6 1.8 %copy-start.10 = (bf16[1024,128]{1,0:T(8,128)(2,1)S(1)}, bf16[1024,128]{1,0:T(8,128)(2,1)}, u32[]{:S(2)}) copy-start(bf16[1024,128]{1,0:T(8,128)(2,1)} %get-tuple-element.47) | copy-start | bytes 786436 | tf_op jit(solution)/shard_map/cond
  55.2 3.6 %copy-start.4 = (f32[1024,128]{1,0:T(8,128)S(1)}, f32[1024,128]{1,0:T(8,128)}, u32[]{:S(2)}) copy-start(f32[1024,128]{1,0:T(8,128)} %copy-done.3) | copy-start | bytes 1572868
  55.2 21.8 %copy-start.6 = (bf16[1,1024,128]{2,1,0:T(8,128)(2,1)S(1)}, bf16[1,1024,128]{2,1,0:T(8,128)(2,1)}, u32[]{:S(2)}) copy-start(bf16[1,1024,128]{2,1,0:T(8,128)(2,1)} %fusion.60) | copy-start | bytes 786436
  55.2 21.7 %collective-permute-start.3 = (bf16[2,1024,128]{2,1,0:T(8,128)(2,1)S(1)}, bf16[2,1024,128]{2,1,0:T(8,128)(2,1)S(1)}, u32[]{:S(2)}, u32[]{:S(2)}) collective-permute-start(bf16[2,1024,128]{2,1,0:T(8,128)(2,1)S(1)} %get-tuple-element.71), channel_id=1, source_target_pairs={{4,0},{8,4},{12,8},{16,12},{20,16},{24,20},{28,24},{32,28},{36,32}... | collective-permute-start | bytes 1572872 | tf_op jit(solution)/shard_map/ppermute | solution.py:15
Sparse Core Ops, SparseCore 0:
  80.7 45.6 reduce-scatter.1
where the time goes:
time: 134 us; the launch traced here: 133 us
  waiting for transfers between devices  68.1 us (51%)
  matrix products  21.7 us (16%)
  starting transfers between devices  18.6 us (14%)
  between operations  17.3 us (13%)
  other arithmetic  4.77 us (4%)
  local copies, waits for them, and re-layouts  2.61 us (2%)
    reduce_scatter x1, waiting for transfers between devices, shards(): lax.psum_scatter(jnp.einsum('crh,cdh->rd', stacked_grads, w_proj, preferr...  45.8 us
    ppermute x6, waiting for transfers between devices, from_behind(): return lax.ppermute(value, axis, pairs)  22.3 us
    ppermute x6, starting transfers between devices, from_behind(): return lax.ppermute(value, axis, pairs)  18.5 us
    dot_general x2, matrix products, tile_task(): jnp.einsum('qh,kh->qk', query_side[1], key_side[1], preferred_element_typ...  7.17 us
    dot_general x2, matrix products, tile_task(): jnp.einsum('qk,qh->kh', weights, query_side[1], preferred_element_type=jn...  5.15 us
    dot_general x2, matrix products, tile_task(): jnp.einsum('qh,kh->qk', query_side[0], key_side[0], preferred_element_typ...  3.39 us
  transfers between devices with their start and end apart: 7, of which 5 were waited for; matrix products, arithmetic and copies ran while one was open for 18% of the time, Pallas kernels for 0%

commit v1 on v0

v1 whole, which is shorter than its diff:
```python
import functools
import math

import jax
import jax.numpy as jnp
from jax import lax
from jax.experimental import pallas as pl
from jax.experimental.pallas import tpu as pltpu
from jax.sharding import PartitionSpec as P

MAXLEN = 3072
CHUNKS = 4
FAR = 8192.0
F32 = jnp.float32
BF16 = jnp.bfloat16
NT = (((1,), (1,)), ((), ()))
NN = (((1,), (0,)), ((), ()))
TN = (((0,), (0,)), ((), ()))


def dot(a, b, dims):
    return lax.dot_general(a, b, dims, preferred_element_type=F32)


def beside(a, b):
    return jnp.concatenate([a, b], axis=1)


def kernel(
    seq_n, head_n,
    q_in, k_in, v_in, g_in, len_in, w_in,
    out_ref,
    kv, qg, ka, qa, dq, dk, dv, gs, gr, wg,
    load_sem, kv_send, qg_send, kv_recv, qg_recv, w_send, w_recv, g_send, g_recv,
):
    rows, width = q_in.shape
    chunk = rows // CHUNKS
    scale = width ** -0.5
    norm = 1.0 / math.sqrt(MAXLEN)
    me = lax.axis_index("seq")
    head = lax.axis_index("head")
    even = lax.rem(me, 2) == 0
    odd = lax.rem(me, 2) == 1

    def at(step):
        return lax.rem(me + step + seq_n, seq_n)

    def other(step):
        return lax.rem(head + step, head_n)

    loads = [
        pltpu.make_async_copy(k_in, kv.at[0, 0], load_sem.at[0]),
        pltpu.make_async_copy(v_in, kv.at[0, 1], load_sem.at[1]),
        pltpu.make_async_copy(q_in, qg.at[0, 0], load_sem.at[2]),
        pltpu.make_async_copy(g_in, qg.at[0, 1], load_sem.at[3]),
    ] + [
        pltpu.make_async_copy(
            w_in.at[c], wg.at[head, :, pl.ds(c * width, width)], load_sem.at[4 + c]
        )
        for c in range(3)
    ]
    for load in loads:
        load.start()

    barrier = pltpu.get_barrier_semaphore()
    for step in (-2, -1, 1, 2):
        pl.semaphore_signal(
            barrier, inc=1, device_id=(at(step), head), device_id_type=pl.DeviceIdType.MESH
        )
    for step in range(1, head_n):
        pl.semaphore_signal(
            barrier, inc=1, device_id=(me, other(step)), device_id_type=pl.DeviceIdType.MESH
        )
    pl.semaphore_wait(barrier, 4 + head_n - 1)

    def send(src, dst, send_sem, recv_sem, seq_to, head_to):
        return pltpu.make_async_remote_copy(
            src_ref=src, dst_ref=dst, send_sem=send_sem, recv_sem=recv_sem,
            device_id=(seq_to, head_to), device_id_type=pl.DeviceIdType.MESH,
        )

    def part(buf, lag, j):
        return buf.at[lag, :, pl.ds(j * chunk, chunk), :]

    def kv_copy(kind, j):
        src, dst, step = ((0, 2, 2), (0, 1, 1), (2, 3, 1), (2, 1, -1))[kind]
        return send(part(kv, src, j), part(kv, dst, j), kv_send.at[kind, j], kv_recv.at[dst, j], at(step), head)

    def qg_copy(kind, j):
        src, dst, step = ((0, 2, -2), (0, 1, -1), (2, 3, -1), (2, 1, 1))[kind]
        return send(part(qg, src, j), part(qg, dst, j), qg_send.at[kind, j], qg_recv.at[dst, j], at(step), head)

    def kv_arrived(lag, j):
        kv_copy({1: 1, 2: 0, 3: 2}[lag], j).wait_recv()

    def qg_arrived(lag, j):
        qg_copy({1: 1, 2: 0, 3: 2}[lag], j).wait_recv()

    for load in loads[:4]:
        load.wait()
    for n in range(CHUNKS):
        kv_copy(0, CHUNKS - 1 - n).start()
        qg_copy(0, n).start()

    @pl.when(even)
    def _():
        for n in range(CHUNKS):
            kv_copy(1, CHUNKS - 1 - n).start()

    @pl.when(odd)
    def _():
        for n in range(CHUNKS):
            qg_copy(1, n).start()

    for load in loads[4:]:
        load.wait()

    def w_copy(step, place):
        return send(wg.at[place], wg.at[place], w_send.at[step - 1], w_recv.at[place], me, other(step))

    for step in range(1, head_n):
        w_copy(step, head).start()

    lane = lax.broadcasted_iota(jnp.int32, (1, width), 1)

    def user_step(u, carry):
        end, starts, ends = carry
        later = end + len_in[u]
        return (later, jnp.where(lane == u, end, starts), jnp.where(lane == u, later, ends))

    zero = jnp.zeros((1, width), jnp.int32)
    _, starts, ends = lax.fori_loop(0, len_in.shape[0], user_step, (jnp.int32(0), zero, zero))
    offsets = lax.broadcasted_iota(jnp.int32, (rows, width), 0)

    def belongs(step):
        pos = offsets + at(step) * rows
        return (pos >= starts) & (pos < ends)

    for lag in range(4):
        ka[lag] = jnp.where(belongs(-lag), 0.0, -FAR).astype(BF16)
        qa[lag] = jnp.where(belongs(lag), 1.0, 0.0).astype(BF16)

    def gates(scores, d_weights):
        s = scores * scale
        p = jax.nn.sigmoid(s)
        a = s * p
        ds = (p + a * (1.0 - p)) * d_weights
        return a.astype(BF16), ds.astype(BF16)

    def query_side(lag, j, r0, r1):
        here = pl.ds(j * chunk, chunk)
        own = slice(r0, r1)
        keys = kv[lag, 0, here, :]
        s = dot(beside(qg[0, 0, own, :], qa[0, own, :]), beside(keys, ka[lag, here, :]), NT)
        d = dot(qg[0, 1, own, :], kv[lag, 1, here, :], NT)
        _, ds = gates(s, d)
        dq[own, :] += dot(ds, keys, NN)

    def key_side(lag, j, r0, r1):
        here = pl.ds(j * chunk, chunk)
        own = slice(r0, r1)
        queries = qg[lag, 0, here, :]
        grads = qg[lag, 1, here, :]
        s = dot(beside(kv[0, 0, own, :], ka[0, own, :]), beside(queries, qa[lag, here, :]), NT)
        d = dot(kv[0, 1, own, :], grads, NT)
        a, ds = gates(s, d)
        dk[own, :] += dot(ds, queries, NN)
        dv[own, :] += dot(a, grads, NN)

    tri = lax.broadcasted_iota(jnp.int32, (chunk, chunk), 0) <= lax.broadcasted_iota(
        jnp.int32, (chunk, chunk), 1
    )
    dk[...] = jnp.zeros_like(dk)
    dv[...] = jnp.zeros_like(dv)
    for j in range(CHUNKS):
        here = slice(j * chunk, (j + 1) * chunk)
        upto = slice(0, (j + 1) * chunk)
        queries = qg[0, 0, here, :]
        grads = qg[0, 1, here, :]
        keys = kv[0, 0, upto, :]
        s = dot(beside(keys, ka[0, upto, :]), beside(queries, qa[0, here, :]), NT)
        last = jnp.where(tri, s[j * chunk :, :], -FAR)
        s = last if j == 0 else jnp.concatenate([s[: j * chunk, :], last], axis=0)
        d = dot(kv[0, 1, upto, :], grads, NT)
        a, ds = gates(s, d)
        dk[upto, :] += dot(ds, queries, NN)
        dv[upto, :] += dot(a, grads, NN)
        dq[here, :] = dot(ds, keys, TN)

    def first(n, _):
        jk, jq = CHUNKS - 1 - n, n
        kv_arrived(2, jk)
        kv_copy(2, jk).start()
        pl.when(odd)(lambda: kv_copy(3, jk).start())
        qg_arrived(2, jq)
        qg_copy(2, jq).start()
        pl.when(even)(lambda: qg_copy(3, jq).start())

        @pl.when(odd)
        def _():
            kv_arrived(1, jk)
            query_side(1, jk, 0, rows)

        @pl.when(even)
        def _():
            qg_arrived(1, jq)
            key_side(1, jq, 0, rows)

        query_side(2, jk, 0, rows)
        key_side(2, jq, 0, rows)
        return 0

    lax.fori_loop(0, CHUNKS, first, 0)

    def second(n, _):
        jk, jq = CHUNKS - 1 - n, n

        @pl.when(even)
        def _():
            kv_arrived(1, jk)
            query_side(1, jk, 0, rows)

        @pl.when(odd)
        def _():
            qg_arrived(1, jq)
            key_side(1, jq, 0, rows)

        return 0

    lax.fori_loop(0, CHUNKS, second, 0)

    wide = {0: (0, 1), 1: (1, 2)}

    def g_copy(which, r, place, to):
        first_col, cols = wide[which]
        span = pl.ds(first_col * width, cols * width)
        return send(
            gs.at[r, :, span], gr.at[place, :, span],
            g_send.at[which, r], g_recv.at[which, place], me, to,
        )

    def hand_over(which, r, value):
        first_col, cols = wide[which]
        span = slice(first_col * width, (first_col + cols) * width)

        @pl.when(head == r)
        def _():
            gr[head, :, span] = value

        @pl.when(head != r)
        def _():
            gs[r, :, span] = value
            g_copy(which, r, head, r).start()

    for n in range(CHUNKS):
        jk, jq = CHUNKS - 1 - n, n
        kv_arrived(3, jk)
        query_side(3, jk, 0, (jk + 1) * chunk)
        own = slice(jk * chunk, (jk + 1) * chunk)
        hand_over(0, jk, (dq[own, :] * (scale * norm)).astype(BF16))
        qg_arrived(3, jq)
        key_side(3, jq, jq * chunk, rows)
        own = slice(jq * chunk, (jq + 1) * chunk)
        hand_over(
            1, jq,
            beside((dk[own, :] * (scale * norm)).astype(BF16), (dv[own, :] * norm).astype(BF16)),
        )

    for step in range(1, head_n):
        w_copy(step, other(head_n - step)).wait_recv()
    total = dot(gr[head], wg[head], NT)
    for step in range(1, head_n):
        place = other(step)
        for which in (0, 1):
            g_copy(which, 0, place, place).wait_recv()
        total += dot(gr[place], wg[place], NT)
    out_ref[...] = total

    for step in range(1, head_n):
        w_copy(step, head).wait_send()
        for which in (0, 1):
            g_copy(which, other(step), head, other(step)).wait_send()
    for j in range(CHUNKS):
        for copy in (kv_copy, qg_copy):
            copy(0, j).wait_send()
            copy(2, j).wait_send()

    @pl.when(even)
    def _():
        for j in range(CHUNKS):
            kv_copy(1, j).wait_send()
            qg_copy(3, j).wait_send()

    @pl.when(odd)
    def _():
        for j in range(CHUNKS):
            kv_copy(3, j).wait_send()
            qg_copy(1, j).wait_send()


def shards(seq_n, head_n, queries, keys, values, out_grad, lengths, w_proj):
    rows, width = queries.shape
    model = w_proj.shape[1]
    hbm = pl.BlockSpec(memory_space=pl.ANY)
    dma = pltpu.SemaphoreType.DMA
    return pl.pallas_call(
        functools.partial(kernel, seq_n, head_n),
        out_shape=jax.ShapeDtypeStruct((rows // head_n, model), F32),
        in_specs=[hbm] * 4 + [pl.BlockSpec(memory_space=pltpu.SMEM), hbm],
        out_specs=pl.BlockSpec(memory_space=pltpu.VMEM),
        scratch_shapes=[
            pltpu.VMEM((4, 2, rows, width), BF16),
            pltpu.VMEM((4, 2, rows, width), BF16),
            pltpu.VMEM((4, rows, width), BF16),
            pltpu.VMEM((4, rows, width), BF16),
            pltpu.VMEM((rows, width), F32),
            pltpu.VMEM((rows, width), F32),
            pltpu.VMEM((rows, width), F32),
            pltpu.VMEM((head_n, rows // head_n, 3 * width), BF16),
            pltpu.VMEM((head_n, rows // head_n, 3 * width), BF16),
            pltpu.VMEM((head_n, model, 3 * width), BF16),
            dma((7,)),
            dma((4, CHUNKS)),
            dma((4, CHUNKS)),
            dma((4, CHUNKS)),
            dma((4, CHUNKS)),
            dma((head_n - 1,)),
            dma((head_n,)),
            dma((2, head_n)),
            dma((2, head_n)),
        ],
        compiler_params=pltpu.CompilerParams(
            collective_id=0, has_side_effects=True, vmem_limit_bytes=48 << 20
        ),
    )(queries, keys, values, out_grad, lengths, w_proj)


def solution(mesh):
    return jax.shard_map(
        functools.partial(shards, mesh.shape["seq"], mesh.shape["head"]),
        mesh=mesh,
        in_specs=(
            P("seq", "head"),
            P("seq", "head"),
            P("seq", "head"),
            P("seq", "head"),
            P(),
            P(None, None, "head"),
        ),
        out_specs=P(("seq", "head"), None),
        check_vma=False,
    )
```

time: 134 us -> 53.6 us (0.40)
  the two profiles are of different devices: /device:TPU:1 before, /device:TPU:6 now
where the time goes in v1:
time: 53.6 us; the launch traced here: 53.4 us
  Pallas kernels  47.1 us (88%)
  local copies, waits for them, and re-layouts  6.24 us (12%)
    pallas_call x1, Pallas kernels, shards(): pl.pallas_call(functools.partial(kernel, seq_n, head_n), out_shape=jax.Sh...  47.1 us
    unnamed x13, local copies, waits for them, and re-layouts  6.24 us

profile of v1, /device:TPU:6, one launch (start us, length us, event | category | flops | bytes accessed | tf_op | source)
XLA Modules:
  0.0 53.4 jit_solution(16080043611666134030)
XLA Ops:
  0.0 0.0 copy-start
  0.0 1.0 %copy-done = bf16[3,512,128]{2,1,0:T(8,128)(2,1)S(1)} copy-done((bf16[3,512,128]{2,1,0:T(8,128)(2,1)S(1)}, bf16[3,512,128]{2,1,0:T(8,128)(2,1)}, u32[]{:S(2)}) %copy-start) | copy-done | bytes 393240
  1.0 0.0 copy-start.1
  1.0 0.9 %copy-done.1 = bf16[1024,128]{1,0:T(8,128)(2,1)S(1)} copy-done((bf16[1024,128]{1,0:T(8,128)(2,1)S(1)}, bf16[1024,128]{1,0:T(8,128)(2,1)}, u32[]{:S(2)}) %copy-start.1) | copy-done | bytes 262168
  1.9 0.0 copy-start.2
  1.9 0.9 %copy-done.2 = bf16[1024,128]{1,0:T(8,128)(2,1)S(1)} copy-done((bf16[1024,128]{1,0:T(8,128)(2,1)S(1)}, bf16[1024,128]{1,0:T(8,128)(2,1)}, u32[]{:S(2)}) %copy-start.2) | copy-done | bytes 262168
  2.9 0.0 copy-start.3
  2.9 0.9 %copy-done.3 = bf16[1024,128]{1,0:T(8,128)(2,1)S(1)} copy-done((bf16[1024,128]{1,0:T(8,128)(2,1)S(1)}, bf16[1024,128]{1,0:T(8,128)(2,1)}, u32[]{:S(2)}) %copy-start.3) | copy-done | bytes 262168
  3.8 0.0 copy-start.4
  3.9 0.9 %copy-done.4 = bf16[1024,128]{1,0:T(8,128)(2,1)S(1)} copy-done((bf16[1024,128]{1,0:T(8,128)(2,1)S(1)}, bf16[1024,128]{1,0:T(8,128)(2,1)}, u32[]{:S(2)}) %copy-start.4) | copy-done | bytes 262168
  4.8 0.0 copy-start.5
  4.8 0.7 %copy-done.5 = s32[64]{0:T(128)S(1)} copy-done((s32[64]{0:T(128)S(1)}, s32[64]{0:T(128)}, u32[]{:S(2)}) %copy-start.5) | copy-done | bytes 280
  5.5 47.1 %shard_map.64 = f32[256,512]{1,0:T(8,128)S(1)} custom-call(bf16[1024,128]{1,0:T(8,128)(2,1)S(1)} %copy-done.1, bf16[1024,128]{1,0:T(8,128)(2,1)S(1)} %copy-done.2, bf16[1024,128]{1,0:T(8,128)(2,1)S(1)} %copy-done.3, bf16[1024,128]{1,0:T(8,128)(2,1)S(1)} %copy-done.4, s32[64]{0:T(128)S(1)} %copy-done.5, bf16[3,512,128]{2,1,0:T(8,128)(2,1)S(1)} %copy-done), custom_call_target="tpu_custom_call" | custom-call | tf_op jit(solution)/shard_map/pallas_call | solution.py:306
  52.6 0.8 %copy.8 = f32[256,512]{1,0:T(8,128)} copy(f32[256,512]{1,0:T(8,128)S(1)} %shard_map.64) | data formatting | bytes 1048576
Async XLA Ops:
  0.0 1.0 %copy-start = (bf16[3,512,128]{2,1,0:T(8,128)(2,1)S(1)}, bf16[3,512,128]{2,1,0:T(8,128)(2,1)}, u32[]{:S(2)}) copy-start(bf16[3,512,128]{2,1,0:T(8,128)(2,1)} %w_in.1) | copy-start | bytes 1179652
  1.0 0.9 %copy-start.1 = (bf16[1024,128]{1,0:T(8,128)(2,1)S(1)}, bf16[1024,128]{1,0:T(8,128)(2,1)}, u32[]{:S(2)}) copy-start(bf16[1024,128]{1,0:T(8,128)(2,1)} %q_in.1) | copy-start | bytes 786436
  1.9 0.9 %copy-start.2 = (bf16[1024,128]{1,0:T(8,128)(2,1)S(1)}, bf16[1024,128]{1,0:T(8,128)(2,1)}, u32[]{:S(2)}) copy-start(bf16[1024,128]{1,0:T(8,128)(2,1)} %k_in.1) | copy-start | bytes 786436
  2.9 0.9 %copy-start.3 = (bf16[1024,128]{1,0:T(8,128)(2,1)S(1)}, bf16[1024,128]{1,0:T(8,128)(2,1)}, u32[]{:S(2)}) copy-start(bf16[1024,128]{1,0:T(8,128)(2,1)} %v_in.1) | copy-start | bytes 786436
  3.8 0.9 %copy-start.4 = (bf16[1024,128]{1,0:T(8,128)(2,1)S(1)}, bf16[1024,128]{1,0:T(8,128)(2,1)}, u32[]{:S(2)}) copy-start(bf16[1024,128]{1,0:T(8,128)(2,1)} %g_in.1) | copy-start | bytes 786436
  4.8 0.7 %copy-start.5 = (s32[64]{0:T(128)S(1)}, s32[64]{0:T(128)}, u32[]{:S(2)}) copy-start(s32[64]{0:T(128)} %len_in.1) | copy-start | bytes 772

commit v2 on v1

v2 whole, which is shorter than its diff:
```python
import functools
import math

import jax
import jax.numpy as jnp
from jax import lax
from jax.experimental import pallas as pl
from jax.experimental.pallas import tpu as pltpu
from jax.sharding import PartitionSpec as P

MAXLEN = 3072
CHUNKS = 4
FAR = 8192.0
F32 = jnp.float32
BF16 = jnp.bfloat16
NT = (((1,), (1,)), ((), ()))
NN = (((1,), (0,)), ((), ()))
TN = (((0,), (0,)), ((), ()))


def dot(a, b, dims):
    return lax.dot_general(a, b, dims, preferred_element_type=F32)


def beside(a, b):
    return jnp.concatenate([a, b], axis=1)


def kernel(
    seq_n, head_n,
    q_in, k_in, v_in, g_in, len_in, w_in,
    out_ref,
    kv, qg, ka, qa, dq, dk, dv, dq_out, dq_in, gs, gr, wg,
    load_sem, qg_send, qg_recv, dq_send, dq_recv, w_send, w_recv, g_send, g_recv,
):
    rows, width = q_in.shape
    chunk = rows // CHUNKS
    scale = width ** -0.5
    norm = 1.0 / math.sqrt(MAXLEN)
    me = lax.axis_index("seq")
    head = lax.axis_index("head")
    even = lax.rem(me, 2) == 0
    odd = lax.rem(me, 2) == 1

    def exists(step):
        return (me + step >= 0) & (me + step < seq_n)

    def other(step):
        return lax.rem(head + step, head_n)

    loads = [
        pltpu.make_async_copy(k_in, kv.at[0], load_sem.at[0]),
        pltpu.make_async_copy(v_in, kv.at[1], load_sem.at[1]),
        pltpu.make_async_copy(q_in, qg.at[0, 0], load_sem.at[2]),
        pltpu.make_async_copy(g_in, qg.at[0, 1], load_sem.at[3]),
    ] + [
        pltpu.make_async_copy(
            w_in.at[c], wg.at[head, :, pl.ds(c * width, width)], load_sem.at[4 + c]
        )
        for c in range(3)
    ]
    for load in loads:
        load.start()

    barrier = pltpu.get_barrier_semaphore()
    for step in (-3, -2, -1, 1, 2, 3):

        @pl.when(exists(step))
        def _():
            pl.semaphore_signal(
                barrier, inc=1, device_id=(me + step, head), device_id_type=pl.DeviceIdType.MESH
            )

    for step in range(1, head_n):
        pl.semaphore_signal(
            barrier, inc=1, device_id=(me, other(step)), device_id_type=pl.DeviceIdType.MESH
        )
    missing = jnp.maximum(3 - me, 0) + jnp.maximum(me + 4 - seq_n, 0)
    pl.semaphore_wait(barrier, 6 + head_n - 1 - missing)

    def send(src, dst, send_sem, recv_sem, seq_to, head_to):
        return pltpu.make_async_remote_copy(
            src_ref=src, dst_ref=dst, send_sem=send_sem, recv_sem=recv_sem,
            device_id=(seq_to, head_to), device_id_type=pl.DeviceIdType.MESH,
        )

    def part(buf, lag, j):
        return buf.at[lag, :, pl.ds(j * chunk, chunk), :]

    def qg_copy(kind, j):
        src, dst, step = ((0, 2, -2), (0, 1, -1), (2, 3, -1), (2, 1, 1))[kind]
        return send(part(qg, src, j), part(qg, dst, j), qg_send.at[kind, j], qg_recv.at[dst, j], me + step, head)

    def qg_arrived(lag, j):
        pl.when(exists(lag))(lambda: qg_copy({1: 1, 2: 0, 3: 2}[lag], j).wait_recv())

    def dq_copy(lag, j):
        here = pl.ds(j * chunk, chunk)
        return send(
            dq_out.at[lag - 1, here, :], dq_in.at[lag - 1, here, :],
            dq_send.at[lag - 1, j], dq_recv.at[lag - 1, j], me + lag, head,
        )

    qg_goes = (exists(-2), odd, exists(2) & exists(-1), even & exists(2))
    for load in loads[2:4]:
        load.wait()
    for n in range(CHUNKS):
        pl.when(qg_goes[0])(lambda: qg_copy(0, n).start())
        pl.when(qg_goes[1])(lambda: qg_copy(1, n).start())
    for load in loads[:2] + loads[4:]:
        load.wait()

    core = lax.rem(me, 2)
    half = w_in.shape[1] // 2
    sibling = me + 1 - 2 * core

    def w_part(place, which):
        return wg.at[place, pl.ds(which * half, half), :]

    def w_copy(step, place):
        ref = w_part(place, core)
        return send(ref, ref, w_send.at[0, step - 1], w_recv.at[0, place], me, other(step))

    def w_share(step, place, which):
        ref = w_part(place, which)
        return send(ref, ref, w_send.at[1, step - 1], w_recv.at[1, place], sibling, head)

    for step in range(1, head_n):
        w_copy(step, head).start()

    lane = lax.broadcasted_iota(jnp.int32, (1, width), 1)

    def user_step(u, carry):
        end, starts, ends = carry
        later = end + len_in[u]
        return (later, jnp.where(lane == u, end, starts), jnp.where(lane == u, later, ends))

    zero = jnp.zeros((1, width), jnp.int32)
    _, starts, ends = lax.fori_loop(0, len_in.shape[0], user_step, (jnp.int32(0), zero, zero))
    offsets = lax.broadcasted_iota(jnp.int32, (rows, width), 0)

    def belongs(step):
        pos = offsets + (me + step) * rows
        return (pos >= starts) & (pos < ends)

    ka[...] = jnp.where(belongs(0), 0.0, -FAR).astype(BF16)
    for lag in range(4):
        qa[lag] = jnp.where(belongs(lag), 1.0, 0.0).astype(BF16)

    for lag in range(1, 4):

        @pl.when(jnp.logical_not(exists(-lag)))
        def _():
            dq_in[lag - 1] = jnp.zeros(dq_in.shape[1:], BF16)

        @pl.when(jnp.logical_not(exists(lag)))
        def _():
            qg[lag] = jnp.zeros(qg.shape[1:], BF16)

    def gates(scores, d_weights):
        s = scores * scale
        p = jax.nn.sigmoid(s)
        a = s * p
        ds = (p + a * (1.0 - p)) * d_weights
        return a.astype(BF16), ds.astype(BF16)

    def terms(lag, j, r0, r1):
        here = pl.ds(j * chunk, chunk)
        own = slice(r0, r1)
        queries = qg[lag, 0, here, :]
        grads = qg[lag, 1, here, :]
        keys = kv[0, own, :]
        s = dot(beside(keys, ka[own, :]), beside(queries, qa[lag, here, :]), NT)
        if lag == 0:
            last = jnp.where(tri, s[r1 - chunk :, :], -FAR)
            s = last if r1 == chunk else jnp.concatenate([s[: r1 - chunk, :], last], axis=0)
        d = dot(kv[1, own, :], grads, NT)
        a, ds = gates(s, d)
        dk[own, :] += dot(ds, queries, NN)
        dv[own, :] += dot(a, grads, NN)
        partial = dot(ds, keys, TN) * (scale * norm)
        if lag == 0:
            dq[here, :] = partial
        else:
            dq_out[lag - 1, here, :] = partial.astype(BF16)
            pl.when(exists(lag))(lambda: dq_copy(lag, j).start())

    tri = lax.broadcasted_iota(jnp.int32, (chunk, chunk), 0) <= lax.broadcasted_iota(
        jnp.int32, (chunk, chunk), 1
    )
    dk[...] = jnp.zeros_like(dk)
    dv[...] = jnp.zeros_like(dv)
    for j in range(CHUNKS):
        terms(0, j, 0, (j + 1) * chunk)

    def step_of(n, _):
        qg_arrived(2, n)
        pl.when(qg_goes[2])(lambda: qg_copy(2, n).start())
        pl.when(qg_goes[3])(lambda: qg_copy(3, n).start())
        terms(2, n, 0, rows)
        qg_arrived(1, n)
        terms(1, n, 0, rows)

        @pl.when(even)
        def _():
            qg_arrived(3, n)
            terms(3, n, 0, rows)

        return 0

    lax.fori_loop(0, CHUNKS, step_of, 0)

    for step in range(1, head_n):
        w_copy(step, other(step)).wait_recv()
        w_share(step, other(step), core).start()

    wide = {0: (0, 1), 1: (1, 2)}

    def g_copy(which, r, place, to):
        first_col, cols = wide[which]
        span = pl.ds(first_col * width, cols * width)
        return send(
            gs.at[r, :, span], gr.at[place, :, span],
            g_send.at[which, r], g_recv.at[which, place], me, to,
        )

    def hand_over(which, r, value):
        first_col, cols = wide[which]
        span = slice(first_col * width, (first_col + cols) * width)

        @pl.when(head == r)
        def _():
            gr[head, :, span] = value

        @pl.when(head != r)
        def _():
            gs[r, :, span] = value
            g_copy(which, r, head, r).start()

    def finish_queries(r):
        own = slice(r * chunk, (r + 1) * chunk)
        total = dq[own, :]
        for lag in range(1, 4):
            pl.when(exists(-lag))(lambda: dq_copy(lag, r).wait_recv())
            total += dq_in[lag - 1, own, :].astype(F32)
        hand_over(0, r, total.astype(BF16))

    def finish_keys(r):
        own = slice(r * chunk, (r + 1) * chunk)
        hand_over(
            1, r,
            beside((dk[own, :] * (scale * norm)).astype(BF16), (dv[own, :] * norm).astype(BF16)),
        )

    @pl.when(even)
    def _():
        for r in range(CHUNKS):
            finish_keys(r)
        for r in range(CHUNKS):
            finish_queries(r)

    @pl.when(odd)
    def _():
        for r in range(CHUNKS):
            qg_arrived(3, r)
            terms(3, r, r * chunk, rows)
            finish_keys(r)
            finish_queries(r)

    for step in range(1, head_n):
        w_share(step, other(step), 1 - core).wait_recv()
    total = dot(gr[head], wg[head], NT)
    for step in range(1, head_n):
        place = other(step)
        for which in (0, 1):
            g_copy(which, 0, place, place).wait_recv()
        total += dot(gr[place], wg[place], NT)
    out_ref[...] = total

    for step in range(1, head_n):
        w_copy(step, head).wait_send()
        w_share(step, other(step), core).wait_send()
        for which in (0, 1):
            g_copy(which, other(step), head, other(step)).wait_send()
    for kind in range(4):

        @pl.when(qg_goes[kind])
        def _():
            for j in range(CHUNKS):
                qg_copy(kind, j).wait_send()

    for lag in range(1, 4):

        @pl.when(exists(lag))
        def _():
            for j in range(CHUNKS):
                dq_copy(lag, j).wait_send()


def shards(seq_n, head_n, queries, keys, values, out_grad, lengths, w_proj):
    rows, width = queries.shape
    model = w_proj.shape[1]
    hbm = pl.BlockSpec(memory_space=pl.ANY)
    dma = pltpu.SemaphoreType.DMA
    return pl.pallas_call(
        functools.partial(kernel, seq_n, head_n),
        out_shape=jax.ShapeDtypeStruct((rows // head_n, model), F32),
        in_specs=[hbm] * 4 + [pl.BlockSpec(memory_space=pltpu.SMEM), hbm],
        out_specs=pl.BlockSpec(memory_space=pltpu.VMEM),
        scratch_shapes=[
            pltpu.VMEM((2, rows, width), BF16),
            pltpu.VMEM((4, 2, rows, width), BF16),
            pltpu.VMEM((rows, width), BF16),
            pltpu.VMEM((4, rows, width), BF16),
            pltpu.VMEM((rows, width), F32),
            pltpu.VMEM((rows, width), F32),
            pltpu.VMEM((rows, width), F32),
            pltpu.VMEM((3, rows, width), BF16),
            pltpu.VMEM((3, rows, width), BF16),
            pltpu.VMEM((head_n, rows // head_n, 3 * width), BF16),
            pltpu.VMEM((head_n, rows // head_n, 3 * width), BF16),
            pltpu.VMEM((head_n, model, 3 * width), BF16),
            dma((7,)),
            dma((4, CHUNKS)),
            dma((4, CHUNKS)),
            dma((3, CHUNKS)),
            dma((3, CHUNKS)),
            dma((2, head_n - 1)),
            dma((2, head_n)),
            dma((2, head_n)),
            dma((2, head_n)),
        ],
        compiler_params=pltpu.CompilerParams(
            collective_id=0, has_side_effects=True, vmem_limit_bytes=60 << 20
        ),
    )(queries, keys, values, out_grad, lengths, w_proj)


def solution(mesh):
    return jax.shard_map(
        functools.partial(shards, mesh.shape["seq"], mesh.shape["head"]),
        mesh=mesh,
        in_specs=(
            P("seq", "head"),
            P("seq", "head"),
            P("seq", "head"),
            P("seq", "head"),
            P(),
            P(None, None, "head"),
        ),
        out_specs=P(("seq", "head"), None),
        check_vma=False,
    )
```

time: 53.6 us -> 46.6 us (0.87)
  the two profiles are of different devices: /device:TPU:6 before, /device:TPU:46 now
where the time goes in v2:
time: 46.6 us; the launch traced here: 46.4 us
  Pallas kernels  44.5 us (95%)
  local copies, waits for them, and re-layouts  1.87 us (4%)
    pallas_call x1, Pallas kernels, shards(): pl.pallas_call(functools.partial(kernel, seq_n, head_n), out_shape=jax.Sh...  44.5 us
    unnamed x1, local copies, waits for them, and re-layouts  1.87 us

profile of v2, /device:TPU:46, one launch (start us, length us, event | category | flops | bytes accessed | tf_op | source)
XLA Modules:
  0.0 46.4 jit_solution(1105554182049992057)
XLA Ops:
  0.0 44.5 %shard_map.64 = f32[256,512]{1,0:T(8,128)} custom-call(bf16[1024,128]{1,0:T(8,128)(2,1)} %q_in.1, bf16[1024,128]{1,0:T(8,128)(2,1)} %k_in.1, bf16[1024,128]{1,0:T(8,128)(2,1)} %v_in.1, bf16[1024,128]{1,0:T(8,128)(2,1)} %g_in.1, s32[64]{0:T(128)} %len_in.1, bf16[3,512,128]{2,1,0:T(8,128)(2,1)} %w_in.1), custom_call_target="tpu_custom_call" | custom-call | tf_op jit(solution)/shard_map/pallas_call | solution.py:305
  44.5 1.9 %copy.8 = f32[256,512]{1,0:T(8,128)} copy(f32[256,512]{1,0:T(8,128)} %shard_map.64) | data formatting | bytes 1048576

commit v3 on v2

--- a/solution.py
+++ b/solution.py
@@ -28,10 +28,10 @@
 
 def kernel(
     seq_n, head_n,
-    q_in, k_in, v_in, g_in, len_in, w_in,
+    q_in, k_in, v_in, g_in, len_hbm, w_in,
     out_ref,
     kv, qg, ka, qa, dq, dk, dv, dq_out, dq_in, gs, gr, wg,
-    load_sem, qg_send, qg_recv, dq_send, dq_recv, w_send, w_recv, g_send, g_recv,
+    load_sem, qg_send, qg_recv, dq_send, dq_recv, w_send, w_recv, g_send, g_recv, len_in,
 ):
     rows, width = q_in.shape
     chunk = rows // CHUNKS
@@ -58,7 +58,7 @@
             w_in.at[c], wg.at[head, :, pl.ds(c * width, width)], load_sem.at[4 + c]
         )
         for c in range(3)
-    ]
+    ] + [pltpu.make_async_copy(len_hbm, len_in, load_sem.at[7])]
     for load in loads:
         load.start()
 
@@ -77,6 +77,9 @@
         )
     missing = jnp.maximum(3 - me, 0) + jnp.maximum(me + 4 - seq_n, 0)
     pl.semaphore_wait(barrier, 6 + head_n - 1 - missing)
+
+    core = lax.rem(me, 2)
+    sibling = me + 1 - 2 * core
 
     def send(src, dst, send_sem, recv_sem, seq_to, head_to):
         return pltpu.make_async_remote_copy(
@@ -98,7 +101,7 @@
         here = pl.ds(j * chunk, chunk)
         return send(
             dq_out.at[lag - 1, here, :], dq_in.at[lag - 1, here, :],
-            dq_send.at[lag - 1, j], dq_recv.at[lag - 1, j], me + lag, head,
+            dq_send.at[lag - 1, j], dq_recv.at[lag - 1, j], sibling if lag == 2 else me + lag, head,
         )
 
     qg_goes = (exists(-2), odd, exists(2) & exists(-1), even & exists(2))
@@ -110,9 +113,7 @@
     for load in loads[:2] + loads[4:]:
         load.wait()
 
-    core = lax.rem(me, 2)
     half = w_in.shape[1] // 2
-    sibling = me + 1 - 2 * core
 
     def w_part(place, which):
         return wg.at[place, pl.ds(which * half, half), :]
@@ -151,7 +152,8 @@
 
         @pl.when(jnp.logical_not(exists(-lag)))
         def _():
-            dq_in[lag - 1] = jnp.zeros(dq_in.shape[1:], BF16)
+            if lag != 2:
+                dq_in[lag - 1] = jnp.zeros(dq_in.shape[1:], BF16)
 
         @pl.when(jnp.logical_not(exists(lag)))
         def _():
@@ -181,9 +183,20 @@
         partial = dot(ds, keys, TN) * (scale * norm)
         if lag == 0:
             dq[here, :] = partial
-        else:
-            dq_out[lag - 1, here, :] = partial.astype(BF16)
-            pl.when(exists(lag))(lambda: dq_copy(lag, j).start())
+            return
+        dq_out[lag - 1, here, :] = partial.astype(BF16)
+        if lag == 2:
+            dq_copy(2, j).start()
+
+    def dq_goes(lag, j):
+        pl.when(exists(lag))(lambda: dq_copy(lag, j).start())
+
+    def dq_joined(lag, j):
+        here = pl.ds(j * chunk, chunk)
+        dq_copy(2, j).wait_recv()
+        total = dq_out[lag - 1, here, :].astype(F32) + dq_in[1, here, :].astype(F32)
+        dq_out[lag - 1, here, :] = total.astype(BF16)
+        dq_goes(lag, j)
 
     tri = lax.broadcasted_iota(jnp.int32, (chunk, chunk), 0) <= lax.broadcasted_iota(
         jnp.int32, (chunk, chunk), 1
@@ -203,8 +216,14 @@
 
         @pl.when(even)
         def _():
+            dq_goes(1, n)
             qg_arrived(3, n)
             terms(3, n, 0, rows)
+            dq_joined(3, n)
+
+        @pl.when(odd)
+        def _():
+            dq_joined(1, n)
 
         return 0
 
@@ -240,7 +259,7 @@
     def finish_queries(r):
         own = slice(r * chunk, (r + 1) * chunk)
         total = dq[own, :]
-        for lag in range(1, 4):
+        for lag in (1, 3):
             pl.when(exists(-lag))(lambda: dq_copy(lag, r).wait_recv())
             total += dq_in[lag - 1, own, :].astype(F32)
         hand_over(0, r, total.astype(BF16))
@@ -264,6 +283,7 @@
         for r in range(CHUNKS):
             qg_arrived(3, r)
             terms(3, r, r * chunk, rows)
+            dq_goes(3, r)
             finish_keys(r)
             finish_queries(r)
 
@@ -289,7 +309,9 @@
             for j in range(CHUNKS):
                 qg_copy(kind, j).wait_send()
 
-    for lag in range(1, 4):
+    for j in range(CHUNKS):
+        dq_copy(2, j).wait_send()
+    for lag in (1, 3):
 
         @pl.when(exists(lag))
         def _():
@@ -302,10 +324,14 @@
     model = w_proj.shape[1]
     hbm = pl.BlockSpec(memory_space=pl.ANY)
     dma = pltpu.SemaphoreType.DMA
+    operands = [
+        pltpu.with_memory_space_constraint(x, pltpu.HBM)
+        for x in (queries, keys, values, out_grad, lengths, w_proj)
+    ]
     return pl.pallas_call(
         functools.partial(kernel, seq_n, head_n),
         out_shape=jax.ShapeDtypeStruct((rows // head_n, model), F32),
-        in_specs=[hbm] * 4 + [pl.BlockSpec(memory_space=pltpu.SMEM), hbm],
+        in_specs=[hbm] * 6,
         out_specs=pl.BlockSpec(memory_space=pltpu.VMEM),
         scratch_shapes=[
             pltpu.VMEM((2, rows, width), BF16),
@@ -320,7 +346,7 @@
             pltpu.VMEM((head_n, rows // head_n, 3 * width), BF16),
             pltpu.VMEM((head_n, rows // head_n, 3 * width), BF16),
             pltpu.VMEM((head_n, model, 3 * width), BF16),
-            dma((7,)),
+            dma((8,)),
             dma((4, CHUNKS)),
             dma((4, CHUNKS)),
             dma((3, CHUNKS)),
@@ -329,11 +355,12 @@
             dma((2, head_n)),
             dma((2, head_n)),
             dma((2, head_n)),
+            pltpu.SMEM(lengths.shape, jnp.int32),
         ],
         compiler_params=pltpu.CompilerParams(
-            collective_id=0, has_side_effects=True, vmem_limit_bytes=60 << 20
+            collective_id=0, has_side_effects=True, vmem_limit_bytes=48 << 20
         ),
-    )(queries, keys, values, out_grad, lengths, w_proj)
+    )(*operands)
 
 
 def solution(mesh):

time: 46.6 us -> 44.1 us (0.946)
  the two profiles are of different devices: /device:TPU:46 before, /device:TPU:62 now
where the time goes in v3:
time: 44.1 us; the launch traced here: 43.9 us
  Pallas kernels  43.1 us (98%)
  local copies, waits for them, and re-layouts  0.8 us (2%)
    pallas_call x1, Pallas kernels, shards(): pl.pallas_call(functools.partial(kernel, seq_n, head_n), out_shape=jax.Sh...  43.1 us

profile of v3, /device:TPU:62, one launch (start us, length us, event | category | flops | bytes accessed | tf_op | source)
XLA Modules:
  0.0 43.9 jit_solution(11892866052383972202)
XLA Ops:
  0.0 43.1 %shard_map.64 = f32[256,512]{1,0:T(8,128)S(1)} custom-call(bf16[1024,128]{1,0:T(8,128)(2,1)} %q_in.1, bf16[1024,128]{1,0:T(8,128)(2,1)} %k_in.1, bf16[1024,128]{1,0:T(8,128)(2,1)} %v_in.1, bf16[1024,128]{1,0:T(8,128)(2,1)} %g_in.1, s32[64]{0:T(128)} %len_hbm.1, bf16[3,512,128]{2,1,0:T(8,128)(2,1)} %w_in.1), custom_call_target="tpu_custom_call" | custom-call | tf_op jit(solution)/shard_map/pallas_call | solution.py:331
  43.1 0.8 %copy.8 = f32[256,512]{1,0:T(8,128)} copy(f32[256,512]{1,0:T(8,128)S(1)} %shard_map.64) | data formatting | bytes 1048576

commit v4 on v3

--- a/solution.py
+++ b/solution.py
@@ -285,6 +285,7 @@
             terms(3, r, r * chunk, rows)
             dq_goes(3, r)
             finish_keys(r)
+        for r in range(CHUNKS):
             finish_queries(r)
 
     for step in range(1, head_n):

time: 44.1 us -> 44 us (level)
  the two profiles are of different devices: /device:TPU:62 before, /device:TPU:46 now
where the time goes in v4:
time: 44 us; the launch traced here: 43.9 us
  Pallas kernels  43.1 us (98%)
  local copies, waits for them, and re-layouts  0.8 us (2%)
    pallas_call x1, Pallas kernels, shards(): pl.pallas_call(functools.partial(kernel, seq_n, head_n), out_shape=jax.Sh...  43.1 us

profile of v4, /device:TPU:46, one launch (start us, length us, event | category | flops | bytes accessed | tf_op | source)
XLA Modules:
  0.0 43.9 jit_solution(18951330713842329)
XLA Ops:
  0.0 43.1 %shard_map.64 = f32[256,512]{1,0:T(8,128)S(1)} custom-call(bf16[1024,128]{1,0:T(8,128)(2,1)} %q_in.1, bf16[1024,128]{1,0:T(8,128)(2,1)} %k_in.1, bf16[1024,128]{1,0:T(8,128)(2,1)} %v_in.1, bf16[1024,128]{1,0:T(8,128)(2,1)} %g_in.1, s32[64]{0:T(128)} %len_hbm.1, bf16[3,512,128]{2,1,0:T(8,128)(2,1)} %w_in.1), custom_call_target="tpu_custom_call" | custom-call | tf_op jit(solution)/shard_map/pallas_call | solution.py:332
  43.1 0.8 %copy.8 = f32[256,512]{1,0:T(8,128)} copy(f32[256,512]{1,0:T(8,128)S(1)} %shard_map.64) | data formatting | bytes 1048576
